TPU v7x, 32 devices: a whole 2x2x4 slice. The times are simulated.
32 devices in a mesh: group: 2 (over x), node: 16 (over z, y, core).
Axes of the slice: x: 2, y: 2, z: 4, core: 2. Of those that a mesh axis runs over, the one named last changes fastest.
Arguments:
- tokens: bfloat16 [512, 7168], P(('group', 'node')), parts along dimension 0, may hold values from -6 to 6
- expert_ids: int32 [512, 4], P(('group', 'node')), parts along dimension 0, may hold values from 0 to 7, as said below
- gates: bfloat16 [512, 4], P(('group', 'node')), parts along dimension 0, may hold values from 0.099609375 to 1
- expert_place: int32 [8], replicated, may hold values from 0 to 7, each once
- gate_proj: bfloat16 [7168, 8192], P(None, 'node'), may hold values from -0.0625 to 0.0625
- up_proj: bfloat16 [7168, 8192], P(None, 'node'), may hold values from -0.0625 to 0.0625
- down_proj: bfloat16 [8192, 7168], P('node'), may hold values from -0.1875 to 0.1875
Outputs:
- moe_out: bfloat16 [512, 7168], P(('group', 'node')), parts along dimension 0
There are 2 independent parts, one for each index of `group`. A program takes and returns all parts, laid end to end along the dimension named above; an argument that names none is the same for every part. Nothing has to cross between parts.
Inputs may be any that keep to these rules, and one draw needn't show every extreme that they name: `expert_ids`: each token names 4 different experts; one expert is named by every token. `expert_place`: each slot holds exactly one expert.
All inputs are finite; a program needn't handle non-finite values.
Results may differ from a plain program's by a relative error of at most 0.005.
Values may be sent and summed in bfloat16 or wider, within the bound.
A program may use at most 128 MiB of HBM per device.

v0:
```python
import jax
import jax.numpy as jnp
from jax import lax
from jax.sharding import PartitionSpec as P


def expert_rows(inputs, w_gate, w_up, w_down):
    gate_part = jnp.dot(inputs, w_gate, preferred_element_type=jnp.float32)
    up_part = jnp.dot(inputs, w_up, preferred_element_type=jnp.float32)
    hidden = (jax.nn.silu(gate_part) * up_part).astype(jnp.bfloat16)
    return jnp.dot(hidden, w_down, preferred_element_type=jnp.float32)


def per_device(tokens, expert_ids, gates, expert_place, gate_proj, up_proj, down_proj):
    chip_count = lax.axis_size("node") // 2
    tok_rows, model_width = tokens.shape
    chip_range = jnp.arange(chip_count, dtype=jnp.int32)
    dest_chip = jnp.sum(
        jnp.where(
            expert_ids[:, :, None] == chip_range[None, None, :], expert_place[None, None, :], 0
        ),
        axis=2,
    )
    chosen = dest_chip[:, :, None] == chip_range[None, None, :]
    weight_tab = jnp.sum(jnp.where(chosen, gates.astype(jnp.float32)[:, :, None], 0.0), axis=1)
    send_mask = jnp.any(chosen, axis=1).T.astype(jnp.bfloat16)
    outgoing = jnp.repeat(send_mask[:, :, None] * tokens[None], 2, axis=0)
    scales = weight_tab.T[:, None, :, None]
    received = lax.all_to_all(outgoing, "node", split_axis=0, concat_axis=0, tiled=True)
    source_count = received.shape[0]
    slot_count = received.shape[1]
    flat = received.reshape(source_count * slot_count, model_width)
    result = lax.all_to_all(
        expert_rows(flat, gate_proj, up_proj, down_proj).reshape(
            source_count, slot_count, model_width
        ),
        "node",
        split_axis=0,
        concat_axis=0,
        tiled=True,
    )
    pieces = result.reshape(chip_count, 2, tok_rows, model_width)
    result = jnp.sum(scales * pieces, axis=(0, 1))
    return result.astype(jnp.bfloat16)


def solution(mesh):
    placed = (
        P(("group", "node"), None),
        P(("group", "node"), None),
        P(("group", "node"), None),
        P(),
        P(None, "node"),
        P(None, "node"),
        P("node", None),
    )
    return jax.shard_map(
        per_device,
        mesh=mesh,
        in_specs=placed,
        out_specs=P(("group", "node"), None),
        check_vma=False,
    )
```

profile of v0, /device:TPU:13, one launch (start us, length us, event | category | flops | bytes accessed | tf_op | source)
XLA Modules:
  0.0 277.1 jit_solution(17871580359134861633)
XLA Ops:
  0.0 0.8 select_reduce_fusion.1
  0.8 0.0 slice-start
  0.8 1.3 broadcast_multiply_fusion
  2.1 0.0 slice-start.1
  2.1 0.5 broadcast_in_dim.40
  2.6 87.5 %all_to_all.10 = bf16[16,16,7168]{2,1,0:T(8,128)(2,1)S(1)} all-to-all(bf16[16,16,7168]{2,1,0:T(8,128)(2,1)S(1)} %bitcast.15), channel_id=1, replica_groups=mesh['group'=2,'node'=16] {'node'}, dimensions={0} | all-to-all | bytes 7340032 | tf_op jit(solution)/shard_map/all_to_all | solution.py:29
  90.1 0.0 copy-start
  90.1 1.9 copy-done
  92.0 0.0 slice-done
  92.0 0.0 slice-done.1
  92.0 2.0 fusion.10
  94.0 13.2 %fusion.1 = f32[256,7168]{1,0:T(8,128)} fusion(bf16[512,7168]{1,0:T(8,128)(2,1)} %param.13, bf16[256,7168]{1,0:T(8,128)(2,1)} %bitcast.13, bf16[7168,512]{1,0:T(8,128)(2,1)} %param.12, f32[256,512]{1,0:T(8,128)S(1)} %fusion.10), kind=kOutput, calls=%fused_computation.4 | convolution fusion | flops 3758882816 | bytes 26214400 | tf_op jit(solution)/shard_map/dot_general | solution.py:11
  107.3 0.0 copy-start.1
  107.3 5.4 %all-to-all-start.1 = ((f32[16,16,7168]{2,1,0:T(8,128)}), f32[16,16,7168]{2,1,0:T(8,128)}, u32[]{:S(2)}, u32[]{:S(2)}) async-start(f32[16,16,7168]{2,1,0:T(8,128)} %bitcast.14), calls=%async_computation.1 | async-start | bytes 14680064 | tf_op jit(solution)/shard_map/all_to_all | solution.py:33
  112.7 0.0 copy-done.1
  112.7 159.8 %all-to-all-done.1 = f32[16,16,7168]{2,1,0:T(8,128)} async-done(((f32[16,16,7168]{2,1,0:T(8,128)}), f32[16,16,7168]{2,1,0:T(8,128)}, u32[]{:S(2)}, u32[]{:S(2)}) %all-to-all-start.1) | async-done | bytes 7340064 | tf_op jit(solution)/shard_map/all_to_all | solution.py:33
  272.5 4.5 %multiply_reduce_fusion = bf16[16,7168]{1,0:T(8,128)(2,1)} fusion(f32[16,16,7168]{2,1,0:T(8,128)} %all-to-all-done.1, f32[16,16]{1,0:T(8,128)S(1)} %bitcast.16), kind=kLoop, calls=%fused_computation | loop fusion | flops 3555328 | bytes 7570432 | tf_op jit(solution)/shard_map/reduce_sum | solution.py:43
  (6 shorter events, 0.0 us)
Async XLA Ops:
  0.8 91.2 %slice-start = ((s8[7340032]{0:T(1024)(128)(4,1)}), s8[4194304]{0:T(1024)(128)(4,1)S(1)}, s32[]{:S(2)}) async-start(s8[7340032]{0:T(1024)(128)(4,1)} %bitcast.18), calls=%async_computation.2 | async-start | bytes 8388608
  2.1 89.9 %slice-start.1 = ((s8[7340032]{0:T(1024)(128)(4,1)}), s8[3145728]{0:T(1024)(128)(4,1)S(1)}, s32[]{:S(2)}) async-start(s8[7340032]{0:T(1024)(128)(4,1)} %bitcast.18), calls=%async_computation.3 | async-start | bytes 6291456
  90.1 1.9 copy-start
  107.3 5.4 %copy-start.1 = (bf16[16,4]{0,1:T(4,128)(2,1)S(1)}, bf16[16,4]{0,1:T(4,128)(2,1)}, u32[]{:S(2)}) copy-start(bf16[16,4]{0,1:T(4,128)(2,1)} %param.9) | copy-start | bytes 388
  107.3 165.2 %all-to-all-start.1 = ((f32[16,16,7168]{2,1,0:T(8,128)}), f32[16,16,7168]{2,1,0:T(8,128)}, u32[]{:S(2)}, u32[]{:S(2)}) async-start(f32[16,16,7168]{2,1,0:T(8,128)} %bitcast.14), calls=%async_computation.1 | async-start | bytes 14680064 | tf_op jit(solution)/shard_map/all_to_all | solution.py:33
where the time goes:
time: 277 us
  waiting for transfers between devices  160 us (58%)
  blocking collectives  87.5 us (32%)
  matrix products  15.3 us (6%)
  other arithmetic  6.64 us (2%)
  starting transfers between devices  5.37 us (2%)
    all_to_all x1, waiting for transfers between devices, per_device(): lax.all_to_all(expert_rows(flat, gate_proj, up_proj, down_proj).reshape(s...  160 us
    all_to_all x1, blocking collectives, per_device(): lax.all_to_all(outgoing, 'node', split_axis=0, concat_axis=0, tiled=True)  87.5 us
    dot_general x1, matrix products, expert_rows(): return jnp.dot(hidden, w_down, preferred_element_type=jnp.float32)  13.2 us
  transfers between devices with their start and end apart: 1, of which 1 were waited for; matrix products, arithmetic and copies ran while one was open for 0% of the time, Pallas kernels for 0%

commit v1 on v0

v1 whole, which is shorter than its diff:
```python
import functools

import jax
import jax.numpy as jnp
from jax import lax
from jax.experimental import pallas as pl
from jax.experimental.pallas import tpu as pltpu
from jax.sharding import PartitionSpec as P

LANES = 128
F32 = jnp.float32
BF16 = jnp.bfloat16


def kernel(
    Z, C,
    place_ref, ids_ref, gates_ref, tokens_ref, wg_hbm, wu_hbm, wd_hbm, out_ref,
    tok, wg, wu, wd, gate_acc, up_acc, hid, own, core_out, core_in, y_out, y_in, z_out, z_in,
    tok_sem, wg_sem, wu_sem, wd_sem,
    az_s, az_r, ay_s, ay_r, ac_s, ac_r,
    rc_s, rc_r, ry_s, ry_r, rz_s, rz_r,
):
    rows, width = tokens_ref.shape
    experts = place_ref.shape[0]
    chunk = width // C
    me = lax.axis_index("node")
    core = lax.rem(me, 2)
    y = lax.rem(me // 2, 2)
    z = me // 4
    core_peer = (z * 2 + y) * 2 + 1 - core
    y_peer = (z * 2 + 1 - y) * 2 + core
    z_peer = [None] + [(lax.rem(z + d, Z) * 2 + y) * 2 + core for d in range(1, Z)]
    quarter = Z * rows
    half = 2 * quarter

    load_tok = pltpu.make_async_copy(tokens_ref, tok.at[0:rows, 0:width], tok_sem)
    load_tok.start()

    barrier = pltpu.get_barrier_semaphore()
    for peer in z_peer[1:] + [y_peer, core_peer]:
        pl.semaphore_signal(barrier, inc=1, device_id={"node": peer})

    ids = ids_ref[...]
    slot_of = jnp.zeros_like(ids)
    for e in range(experts):
        slot_of = slot_of + jnp.where(ids == e, place_ref[e], 0)
    gates = gates_ref[...].astype(F32)
    lane = lax.broadcasted_iota(jnp.int32, (rows, LANES), 1)
    table = jnp.zeros((rows, LANES), F32)
    for k in range(ids.shape[1]):
        table = table + jnp.where(slot_of[:, k:k + 1] == lane, gates[:, k:k + 1], 0.0)
    tok[0:rows, width:width + LANES] = table.astype(BF16)

    def cols(c):
        return pl.ds(c * chunk, chunk)

    def cols_tab(c):
        return pl.ds(c * chunk, chunk + (LANES if c == C - 1 else 0))

    def remote(src, dst, send, recv, peer):
        return pltpu.make_async_remote_copy(
            src_ref=src, dst_ref=dst, send_sem=send, recv_sem=recv,
            device_id={"node": peer}, device_id_type=pl.DeviceIdType.MESH,
        )

    load_tok.wait()
    pl.semaphore_wait(barrier, Z + 1)

    gz, gy, gc = [], [], []
    for c in range(C):
        own_block = tok.at[0:rows, cols_tab(c)]
        gz.append([
            remote(own_block, tok.at[(Z - d) * rows:(Z - d + 1) * rows, cols_tab(c)],
                   az_s.at[c, d], az_r.at[c, Z - d], z_peer[d])
            for d in range(1, Z)
        ])
        gy.append(remote(tok.at[0:quarter, cols_tab(c)], tok.at[quarter:half, cols_tab(c)],
                         ay_s.at[c], ay_r.at[c], y_peer))
        gc.append([
            remote(tok.at[h * quarter:(h + 1) * quarter, cols_tab(c)],
                   tok.at[half + h * quarter:half + (h + 1) * quarter, cols_tab(c)],
                   ac_s.at[c, h], ac_r.at[c, h], core_peer)
            for h in range(2)
        ])
    for c in range(C):
        for copy in gz[c]:
            copy.start()
    loads = []
    for c in range(C):
        loads.append([
            pltpu.make_async_copy(wg_hbm.at[cols(c), :], wg.at[cols(c), :], wg_sem.at[c]),
            pltpu.make_async_copy(wu_hbm.at[cols(c), :], wu.at[cols(c), :], wu_sem.at[c]),
        ])
        for copy in loads[c]:
            copy.start()
    load_down = [
        pltpu.make_async_copy(wd_hbm.at[:, cols(c)], wd.at[:, cols(c)], wd_sem.at[c])
        for c in range(C)
    ]
    for copy in load_down:
        copy.start()

    for step in range(C + 2):
        if step < C:
            c = step
            for copy in gz[c]:
                copy.wait_recv()
            gy[c].start()
            gc[c][0].start()
        if 0 <= step - 1 < C:
            c = step - 1
            gy[c].wait_recv()
            gc[c][1].start()
        if 0 <= step - 2 < C:
            c = step - 2
            for copy in loads[c]:
                copy.wait()
            for copy in gc[c]:
                copy.wait_recv()
            x = tok[:, cols(c)]
            gate_part = jnp.dot(x, wg[cols(c), :], preferred_element_type=F32)
            up_part = jnp.dot(x, wu[cols(c), :], preferred_element_type=F32)
            if c == 0:
                gate_acc[...] = gate_part
                up_acc[...] = up_part
            elif c < C - 1:
                gate_acc[...] += gate_part
                up_acc[...] += up_part
            else:
                gate_part = gate_acc[...] + gate_part
                up_part = up_acc[...] + up_part
                hid[...] = (jax.nn.silu(gate_part) * up_part).astype(BF16)

    all_rows = 2 * half
    lane = lax.broadcasted_iota(jnp.int32, (all_rows, LANES), 1)
    scale = jnp.sum(
        jnp.where(lane == me // 2, tok[:, width:width + LANES].astype(F32), 0.0),
        axis=1, keepdims=True,
    )

    sc = [remote(core_out.at[:, cols(c)], core_in.at[:, cols(c)], rc_s.at[c], rc_r.at[c], core_peer)
          for c in range(C)]
    sy = [remote(y_out.at[:, cols(c)], y_in.at[:, cols(c)], ry_s.at[c], ry_r.at[c], y_peer)
          for c in range(C)]
    sz = [[remote(z_out.at[d * rows:(d + 1) * rows, cols(c)],
                  z_in.at[(Z - d) * rows:(Z - d + 1) * rows, cols(c)],
                  rz_s.at[c, d], rz_r.at[c, Z - d], z_peer[d]) for d in range(1, Z)]
          for c in range(C)]

    for step in range(C + 3):
        if step < C:
            c = step
            load_down[c].wait()
            part = scale * jnp.dot(hid[...], wd[:, cols(c)], preferred_element_type=F32)
            core_out[:, cols(c)] = part[half:].astype(BF16)
            sc[c].start()
            own[:, cols(c)] = part[:half]
        if 0 <= step - 1 < C:
            c = step - 1
            sc[c].wait_recv()
            total = own[:, cols(c)] + core_in[:, cols(c)].astype(F32)
            y_out[:, cols(c)] = total[quarter:].astype(BF16)
            sy[c].start()
            own[0:quarter, cols(c)] = total[:quarter]
        if 0 <= step - 2 < C:
            c = step - 2
            sy[c].wait_recv()
            total = own[0:quarter, cols(c)] + y_in[:, cols(c)].astype(F32)
            z_out[rows:, cols(c)] = total[rows:].astype(BF16)
            for copy in sz[c]:
                copy.start()
            own[0:rows, cols(c)] = total[:rows]
        if 0 <= step - 3 < C:
            c = step - 3
            for copy in sz[c]:
                copy.wait_recv()
            total = own[0:rows, cols(c)]
            for d in range(1, Z):
                total = total + z_in[d * rows:(d + 1) * rows, cols(c)].astype(F32)
            out_ref[:, cols(c)] = total.astype(BF16)

    for c in range(C):
        for copy in gz[c] + [gy[c]] + gc[c] + [sc[c], sy[c]] + sz[c]:
            copy.wait_send()


def per_device(tokens, expert_ids, gates, expert_place, gate_proj, up_proj, down_proj):
    nodes = lax.axis_size("node")
    Z = nodes // 4
    C = 7
    rows, width = tokens.shape
    units = gate_proj.shape[1]
    all_rows = nodes * rows
    dma = pltpu.SemaphoreType.DMA
    vmem = pl.BlockSpec(memory_space=pltpu.VMEM)
    hbm = pl.BlockSpec(memory_space=pl.ANY)
    return pl.pallas_call(
        functools.partial(kernel, Z, C),
        out_shape=jax.ShapeDtypeStruct((rows, width), BF16),
        in_specs=[pl.BlockSpec(memory_space=pltpu.SMEM), vmem, vmem, hbm, hbm, hbm, hbm],
        out_specs=vmem,
        scratch_shapes=[
            pltpu.VMEM((all_rows, width + LANES), BF16),
            pltpu.VMEM((width, units), BF16),
            pltpu.VMEM((width, units), BF16),
            pltpu.VMEM((units, width), BF16),
            pltpu.VMEM((all_rows, units), F32),
            pltpu.VMEM((all_rows, units), F32),
            pltpu.VMEM((all_rows, units), BF16),
            pltpu.VMEM((all_rows // 2, width), F32),
            pltpu.VMEM((all_rows // 2, width), BF16),
            pltpu.VMEM((all_rows // 2, width), BF16),
            pltpu.VMEM((all_rows // 4, width), BF16),
            pltpu.VMEM((all_rows // 4, width), BF16),
            pltpu.VMEM((all_rows // 4, width), BF16),
            pltpu.VMEM((all_rows // 4, width), BF16),
            dma, dma((C,)), dma((C,)), dma((C,)),
            dma((C, Z)), dma((C, Z)), dma((C,)), dma((C,)), dma((C, 2)), dma((C, 2)),
            dma((C,)), dma((C,)), dma((C,)), dma((C,)), dma((C, Z)), dma((C, Z)),
        ],
        compiler_params=pltpu.CompilerParams(
            collective_id=0, has_side_effects=True, vmem_limit_bytes=60 * 2 ** 20
        ),
        cost_estimate=pl.CostEstimate(
            flops=6 * all_rows * width * units,
            bytes_accessed=6 * width * units,
            transcendentals=all_rows * units,
        ),
    )(expert_place, expert_ids, gates, tokens, gate_proj, up_proj, down_proj)


def solution(mesh):
    placed = (
        P(("group", "node"), None),
        P(("group", "node"), None),
        P(("group", "node"), None),
        P(),
        P(None, "node"),
        P(None, "node"),
        P("node", None),
    )
    return jax.shard_map(
        per_device,
        mesh=mesh,
        in_specs=placed,
        out_specs=P(("group", "node"), None),
        check_vma=False,
    )
```

time: 277 us -> 76.2 us (0.28)
  the two profiles are of different devices: /device:TPU:13 before, /device:TPU:0 now
where the time goes in v1:
time: 76.2 us; the launch traced here: 75.9 us
  Pallas kernels  71.6 us (94%)
  local copies, waits for them, and re-layouts  4.34 us (6%)
    pallas_call x1, Pallas kernels, per_device(): pl.pallas_call(functools.partial(kernel, Z, C), out_shape=jax.ShapeDtypeS...  71.6 us
    unnamed x3, local copies, waits for them, and re-layouts  4.34 us

profile of v1, /device:TPU:0, one launch (start us, length us, event | category | flops | bytes accessed | tf_op | source)
XLA Modules:
  0.0 75.9 jit_solution(8445239130260298309)
XLA Ops:
  0.0 1.3 %copy.9.gates_ref = bf16[16,4]{1,0:T(8,128)(2,1)} copy(bf16[16,4]{0,1:T(4,128)(2,1)} %param.9) | data formatting | bytes 256 | tf_op args[2]
  1.3 1.4 %copy.8.ids_ref = s32[16,4]{1,0:T(8,128)} copy(s32[16,4]{0,1:T(4,128)} %param.8) | data formatting | bytes 512 | tf_op args[1]
  2.7 71.6 %shard_map.73 = bf16[16,7168]{1,0:T(8,128)(2,1)} custom-call(s32[8]{0:T(128)} %place_ref.1, s32[16,4]{1,0:T(8,128)} %copy.8.ids_ref, bf16[16,4]{1,0:T(8,128)(2,1)} %copy.9.gates_ref, bf16[16,7168]{1,0:T(8,128)(2,1)} %tokens_ref.1, bf16[7168,512]{1,0:T(8,128)(2,1)} %wg_hbm.1, bf16[7168,512]{1,0:T(8,128)(2,1)} %wu_hbm.1, bf16[512,7168]{1,0:T(8,128)(2,1)} %wd_hbm.1), custom_call_target="tpu_custom_call" | custom-call | flops 5637144576 | bytes 22020096 | tf_op jit(solution)/shard_map/pallas_call | solution.py:197
  74.3 1.6 %copy.11 = bf16[16,7168]{1,0:T(8,128)(2,1)} copy(bf16[16,7168]{1,0:T(8,128)(2,1)} %shard_map.73) | data formatting | bytes 458752

commit v2 on v1

--- a/solution.py
+++ b/solution.py
@@ -17,8 +17,8 @@
     place_ref, ids_ref, gates_ref, tokens_ref, wg_hbm, wu_hbm, wd_hbm, out_ref,
     tok, wg, wu, wd, gate_acc, up_acc, hid, own, core_out, core_in, y_out, y_in, z_out, z_in,
     tok_sem, wg_sem, wu_sem, wd_sem,
-    az_s, az_r, ay_s, ay_r, ac_s, ac_r,
-    rc_s, rc_r, ry_s, ry_r, rz_s, rz_r,
+    az_s, az_r, ao_s, ao_r, ay_s, ay_r, ac_s, ac_r,
+    rc_s, rc_r, ro_s, ro_r, ry_s, ry_r, rz_s, rz_r,
 ):
     rows, width = tokens_ref.shape
     experts = place_ref.shape[0]
@@ -40,17 +40,6 @@
     for peer in z_peer[1:] + [y_peer, core_peer]:
         pl.semaphore_signal(barrier, inc=1, device_id={"node": peer})
 
-    ids = ids_ref[...]
-    slot_of = jnp.zeros_like(ids)
-    for e in range(experts):
-        slot_of = slot_of + jnp.where(ids == e, place_ref[e], 0)
-    gates = gates_ref[...].astype(F32)
-    lane = lax.broadcasted_iota(jnp.int32, (rows, LANES), 1)
-    table = jnp.zeros((rows, LANES), F32)
-    for k in range(ids.shape[1]):
-        table = table + jnp.where(slot_of[:, k:k + 1] == lane, gates[:, k:k + 1], 0.0)
-    tok[0:rows, width:width + LANES] = table.astype(BF16)
-
     def cols(c):
         return pl.ds(c * chunk, chunk)
 
@@ -66,7 +55,7 @@
     load_tok.wait()
     pl.semaphore_wait(barrier, Z + 1)
 
-    gz, gy, gc = [], [], []
+    gz, go, gy, gc = [], [], [], []
     for c in range(C):
         own_block = tok.at[0:rows, cols_tab(c)]
         gz.append([
@@ -74,7 +63,10 @@
                    az_s.at[c, d], az_r.at[c, Z - d], z_peer[d])
             for d in range(1, Z)
         ])
-        gy.append(remote(tok.at[0:quarter, cols_tab(c)], tok.at[quarter:half, cols_tab(c)],
+        go.append(remote(own_block, tok.at[quarter:quarter + rows, cols_tab(c)],
+                         ao_s.at[c], ao_r.at[c], y_peer))
+        gy.append(remote(tok.at[rows:quarter, cols_tab(c)],
+                         tok.at[quarter + rows:half, cols_tab(c)],
                          ay_s.at[c], ay_r.at[c], y_peer))
         gc.append([
             remote(tok.at[h * quarter:(h + 1) * quarter, cols_tab(c)],
@@ -82,9 +74,11 @@
                    ac_s.at[c, h], ac_r.at[c, h], core_peer)
             for h in range(2)
         ])
-    for c in range(C):
-        for copy in gz[c]:
+    for c in range(2):
+        for copy in gz[c] + [go[c]]:
             copy.start()
+    for c in range(2, C - 1):
+        go[c].start()
     loads = []
     for c in range(C):
         loads.append([
@@ -100,6 +94,18 @@
     for copy in load_down:
         copy.start()
 
+    ids = ids_ref[...]
+    slot_of = jnp.zeros_like(ids)
+    for e in range(experts):
+        slot_of = slot_of + jnp.where(ids == e, place_ref[e], 0)
+    gates = gates_ref[...].astype(F32)
+    slot = lax.broadcasted_iota(jnp.int32, (LANES, rows), 0)
+    table = jnp.zeros((LANES, rows), F32)
+    for k in range(ids.shape[0]):
+        table = table + jnp.where(slot_of[k:k + 1, :] == slot, gates[k:k + 1, :], 0.0)
+    tok[0:rows, width:width + LANES] = table.T.astype(BF16)
+    go[C - 1].start()
+
     for step in range(C + 2):
         if step < C:
             c = step
@@ -107,8 +113,12 @@
                 copy.wait_recv()
             gy[c].start()
             gc[c][0].start()
+            if c + 2 < C:
+                for copy in gz[c + 2]:
+                    copy.start()
         if 0 <= step - 1 < C:
             c = step - 1
+            go[c].wait_recv()
             gy[c].wait_recv()
             gc[c][1].start()
         if 0 <= step - 2 < C:
@@ -140,14 +150,16 @@
 
     sc = [remote(core_out.at[:, cols(c)], core_in.at[:, cols(c)], rc_s.at[c], rc_r.at[c], core_peer)
           for c in range(C)]
-    sy = [remote(y_out.at[:, cols(c)], y_in.at[:, cols(c)], ry_s.at[c], ry_r.at[c], y_peer)
-          for c in range(C)]
+    so = [remote(y_out.at[0:rows, cols(c)], y_in.at[0:rows, cols(c)],
+                 ro_s.at[c], ro_r.at[c], y_peer) for c in range(C)]
+    sy = [remote(y_out.at[rows:quarter, cols(c)], y_in.at[rows:quarter, cols(c)],
+                 ry_s.at[c], ry_r.at[c], y_peer) for c in range(C)]
     sz = [[remote(z_out.at[d * rows:(d + 1) * rows, cols(c)],
                   z_in.at[(Z - d) * rows:(Z - d + 1) * rows, cols(c)],
                   rz_s.at[c, d], rz_r.at[c, Z - d], z_peer[d]) for d in range(1, Z)]
           for c in range(C)]
 
-    for step in range(C + 3):
+    for step in range(C + 2):
         if step < C:
             c = step
             load_down[c].wait()
@@ -162,25 +174,27 @@
             y_out[:, cols(c)] = total[quarter:].astype(BF16)
             sy[c].start()
             own[0:quarter, cols(c)] = total[:quarter]
+            if c == C - 1:
+                for copy in so:
+                    copy.start()
         if 0 <= step - 2 < C:
             c = step - 2
             sy[c].wait_recv()
-            total = own[0:quarter, cols(c)] + y_in[:, cols(c)].astype(F32)
-            z_out[rows:, cols(c)] = total[rows:].astype(BF16)
+            total = own[rows:quarter, cols(c)] + y_in[rows:, cols(c)].astype(F32)
+            z_out[rows:, cols(c)] = total.astype(BF16)
             for copy in sz[c]:
                 copy.start()
-            own[0:rows, cols(c)] = total[:rows]
-        if 0 <= step - 3 < C:
-            c = step - 3
-            for copy in sz[c]:
-                copy.wait_recv()
-            total = own[0:rows, cols(c)]
-            for d in range(1, Z):
-                total = total + z_in[d * rows:(d + 1) * rows, cols(c)].astype(F32)
-            out_ref[:, cols(c)] = total.astype(BF16)
-
-    for c in range(C):
-        for copy in gz[c] + [gy[c]] + gc[c] + [sc[c], sy[c]] + sz[c]:
+    for c in range(C):
+        so[c].wait_recv()
+        for copy in sz[c]:
+            copy.wait_recv()
+        total = own[0:rows, cols(c)] + y_in[0:rows, cols(c)].astype(F32)
+        for d in range(1, Z):
+            total = total + z_in[d * rows:(d + 1) * rows, cols(c)].astype(F32)
+        out_ref[:, cols(c)] = total.astype(BF16)
+
+    for c in range(C):
+        for copy in gz[c] + [go[c], gy[c]] + gc[c] + [sc[c], so[c], sy[c]] + sz[c]:
             copy.wait_send()
 
 
@@ -215,8 +229,8 @@
             pltpu.VMEM((all_rows // 4, width), BF16),
             pltpu.VMEM((all_rows // 4, width), BF16),
             dma, dma((C,)), dma((C,)), dma((C,)),
-            dma((C, Z)), dma((C, Z)), dma((C,)), dma((C,)), dma((C, 2)), dma((C, 2)),
-            dma((C,)), dma((C,)), dma((C,)), dma((C,)), dma((C, Z)), dma((C, Z)),
+            dma((C, Z)), dma((C, Z)), dma((C,)), dma((C,)), dma((C,)), dma((C,)), dma((C, 2)), dma((C, 2)),
+            dma((C,)), dma((C,)), dma((C,)), dma((C,)), dma((C,)), dma((C,)), dma((C, Z)), dma((C, Z)),
         ],
         compiler_params=pltpu.CompilerParams(
             collective_id=0, has_side_effects=True, vmem_limit_bytes=60 * 2 ** 20
@@ -226,7 +240,7 @@
             bytes_accessed=6 * width * units,
             transcendentals=all_rows * units,
         ),
-    )(expert_place, expert_ids, gates, tokens, gate_proj, up_proj, down_proj)
+    )(expert_place, expert_ids.T, gates.T, tokens, gate_proj, up_proj, down_proj)
 
 
 def solution(mesh):

time: 76.2 us -> 64.6 us (0.85)
  Pallas kernels: 71.6 us -> 62.7 us
  local copies, waits for them, and re-layouts: 4.34 us -> 1.64 us
    pallas_call x1, Pallas kernels: 71.6 us -> 62.7 us  [per_device(): pl.pallas_call(functools.partial(kernel, Z, C), out_shape=jax.ShapeDtypeS...]
    unnamed x3 -> x1, local copies, waits for them, and re-layouts: 4.34 us -> 1.64 us
where the time goes in v2:
time: 64.6 us; the launch traced here: 64.4 us
  Pallas kernels  62.7 us (97%)
  local copies, waits for them, and re-layouts  1.64 us (3%)
    pallas_call x1, Pallas kernels, per_device(): pl.pallas_call(functools.partial(kernel, Z, C), out_shape=jax.ShapeDtypeS...  62.7 us
    unnamed x1, local copies, waits for them, and re-layouts  1.64 us

profile of v2, /device:TPU:0, one launch (start us, length us, event | category | flops | bytes accessed | tf_op | source)
XLA Modules:
  0.0 64.4 jit_solution(9747936506530155997)
XLA Ops:
  0.0 62.7 %shard_map.73 = bf16[16,7168]{1,0:T(8,128)(2,1)} custom-call(s32[8]{0:T(128)} %place_ref.1, s32[4,16]{1,0:T(4,128)} %bitcast.2, bf16[4,16]{1,0:T(4,128)(2,1)} %bitcast.3, bf16[16,7168]{1,0:T(8,128)(2,1)} %tokens_ref.1, bf16[7168,512]{1,0:T(8,128)(2,1)} %wg_hbm.1, bf16[7168,512]{1,0:T(8,128)(2,1)} %wu_hbm.1, bf16[512,7168]{1,0:T(8,128)(2,1)} %wd_hbm.1), custom_call_target="tpu_custom_call" | custom-call | flops 5637144576 | bytes 22020096 | tf_op jit(solution)/shard_map/pallas_call | solution.py:211
  62.8 1.6 %copy.9 = bf16[16,7168]{1,0:T(8,128)(2,1)} copy(bf16[16,7168]{1,0:T(8,128)(2,1)} %shard_map.73) | data formatting | bytes 458752

commit v3 on v2

--- a/solution.py
+++ b/solution.py
@@ -17,7 +17,7 @@
     place_ref, ids_ref, gates_ref, tokens_ref, wg_hbm, wu_hbm, wd_hbm, out_ref,
     tok, wg, wu, wd, gate_acc, up_acc, hid, own, core_out, core_in, y_out, y_in, z_out, z_in,
     tok_sem, wg_sem, wu_sem, wd_sem,
-    az_s, az_r, ao_s, ao_r, ay_s, ay_r, ac_s, ac_r,
+    az_s, az_r, al_s, ao_s, ao_r, ay_s, ay_r, ac_s, ac_r,
     rc_s, rc_r, ro_s, ro_r, ry_s, ry_r, rz_s, rz_r,
 ):
     rows, width = tokens_ref.shape
@@ -63,22 +63,47 @@
                    az_s.at[c, d], az_r.at[c, Z - d], z_peer[d])
             for d in range(1, Z)
         ])
-        go.append(remote(own_block, tok.at[quarter:quarter + rows, cols_tab(c)],
-                         ao_s.at[c], ao_r.at[c], y_peer))
         gy.append(remote(tok.at[rows:quarter, cols_tab(c)],
                          tok.at[quarter + rows:half, cols_tab(c)],
                          ay_s.at[c], ay_r.at[c], y_peer))
-        gc.append([
-            remote(tok.at[h * quarter:(h + 1) * quarter, cols_tab(c)],
-                   tok.at[half + h * quarter:half + (h + 1) * quarter, cols_tab(c)],
-                   ac_s.at[c, h], ac_r.at[c, h], core_peer)
-            for h in range(2)
-        ])
-    for c in range(2):
-        for copy in gz[c] + [go[c]]:
-            copy.start()
-    for c in range(2, C - 1):
-        go[c].start()
+        gc.append(remote(tok.at[0:half, cols_tab(c)], tok.at[half:2 * half, cols_tab(c)],
+                         ac_s.at[c], ac_r.at[c], core_peer))
+    split = C // 2 + 1
+    for g, span in enumerate([
+        pl.ds(0, split * chunk), pl.ds(split * chunk, (C - split) * chunk + LANES)
+    ]):
+        go.append(remote(tok.at[0:rows, span], tok.at[quarter:quarter + rows, span],
+                         ao_s.at[g], ao_r.at[g], y_peer))
+    relayed = Z == 4
+    relay = [
+        (remote(tok.at[2 * rows:3 * rows, cols_tab(c)], tok.at[3 * rows:4 * rows, cols_tab(c)],
+                al_s.at[c], az_r.at[c, 3], z_peer[3]),
+         remote(tok.at[2 * rows:3 * rows, cols_tab(c)], tok.at[rows:2 * rows, cols_tab(c)],
+                al_s.at[c], az_r.at[c, 1], z_peer[1]))
+        for c in range(C)
+    ] if relayed else []
+
+    def each_z(c, act):
+        for d in [2, 1] + list(range(3, Z)):
+            if relayed and d != 2:
+                pl.when(z != (3 if d == 1 else 0))(functools.partial(act, gz[c][d - 1]))
+            else:
+                act(gz[c][d - 1])
+
+    def each_relay(c, act):
+        for at, copy in enumerate(relay[c] if relayed else ()):
+            pl.when(z == at + 1)(functools.partial(act, copy))
+
+    def start(copy):
+        copy.start()
+
+    def wait_send(copy):
+        copy.wait_send()
+
+    each_z(0, start)
+    go[0].start()
+    for c in range(1, 3):
+        each_z(c, start)
     loads = []
     for c in range(C):
         loads.append([
@@ -104,29 +129,29 @@
     for k in range(ids.shape[0]):
         table = table + jnp.where(slot_of[k:k + 1, :] == slot, gates[k:k + 1, :], 0.0)
     tok[0:rows, width:width + LANES] = table.T.astype(BF16)
-    go[C - 1].start()
+    go[1].start()
 
     for step in range(C + 2):
         if step < C:
             c = step
-            for copy in gz[c]:
+            gz[c][1].wait_recv()
+            each_relay(c, start)
+            for copy in gz[c][0:1] + gz[c][2:]:
                 copy.wait_recv()
             gy[c].start()
-            gc[c][0].start()
-            if c + 2 < C:
-                for copy in gz[c + 2]:
-                    copy.start()
+            if c + 3 < C:
+                each_z(c + 3, start)
         if 0 <= step - 1 < C:
             c = step - 1
-            go[c].wait_recv()
+            if c in (0, split):
+                go[c // split].wait_recv()
             gy[c].wait_recv()
-            gc[c][1].start()
+            gc[c].start()
         if 0 <= step - 2 < C:
             c = step - 2
             for copy in loads[c]:
                 copy.wait()
-            for copy in gc[c]:
-                copy.wait_recv()
+            gc[c].wait_recv()
             x = tok[:, cols(c)]
             gate_part = jnp.dot(x, wg[cols(c), :], preferred_element_type=F32)
             up_part = jnp.dot(x, wu[cols(c), :], preferred_element_type=F32)
@@ -150,8 +175,10 @@
 
     sc = [remote(core_out.at[:, cols(c)], core_in.at[:, cols(c)], rc_s.at[c], rc_r.at[c], core_peer)
           for c in range(C)]
-    so = [remote(y_out.at[0:rows, cols(c)], y_in.at[0:rows, cols(c)],
-                 ro_s.at[c], ro_r.at[c], y_peer) for c in range(C)]
+    so = [remote(y_out.at[0:rows, span], y_in.at[0:rows, span], ro_s.at[g], ro_r.at[g], y_peer)
+          for g, span in enumerate([
+              pl.ds(0, split * chunk), pl.ds(split * chunk, (C - split) * chunk)
+          ])]
     sy = [remote(y_out.at[rows:quarter, cols(c)], y_in.at[rows:quarter, cols(c)],
                  ry_s.at[c], ry_r.at[c], y_peer) for c in range(C)]
     sz = [[remote(z_out.at[d * rows:(d + 1) * rows, cols(c)],
@@ -185,7 +212,8 @@
             for copy in sz[c]:
                 copy.start()
     for c in range(C):
-        so[c].wait_recv()
+        if c in (0, split):
+            so[c // split].wait_recv()
         for copy in sz[c]:
             copy.wait_recv()
         total = own[0:rows, cols(c)] + y_in[0:rows, cols(c)].astype(F32)
@@ -194,8 +222,12 @@
         out_ref[:, cols(c)] = total.astype(BF16)
 
     for c in range(C):
-        for copy in gz[c] + [go[c], gy[c]] + gc[c] + [sc[c], so[c], sy[c]] + sz[c]:
+        each_z(c, wait_send)
+        each_relay(c, wait_send)
+        for copy in [gy[c], gc[c], sc[c], sy[c]] + sz[c]:
             copy.wait_send()
+    for copy in go + so:
+        copy.wait_send()
 
 
 def per_device(tokens, expert_ids, gates, expert_place, gate_proj, up_proj, down_proj):
@@ -229,8 +261,9 @@
             pltpu.VMEM((all_rows // 4, width), BF16),
             pltpu.VMEM((all_rows // 4, width), BF16),
             dma, dma((C,)), dma((C,)), dma((C,)),
-            dma((C, Z)), dma((C, Z)), dma((C,)), dma((C,)), dma((C,)), dma((C,)), dma((C, 2)), dma((C, 2)),
-            dma((C,)), dma((C,)), dma((C,)), dma((C,)), dma((C,)), dma((C,)), dma((C, Z)), dma((C, Z)),
+            dma((C, Z)), dma((C, Z)), dma((C,)), dma((2,)), dma((2,)),
+            dma((C,)), dma((C,)), dma((C,)), dma((C,)),
+            dma((C,)), dma((C,)), dma((2,)), dma((2,)), dma((C,)), dma((C,)), dma((C, Z)), dma((C, Z)),
         ],
         compiler_params=pltpu.CompilerParams(
             collective_id=0, has_side_effects=True, vmem_limit_bytes=60 * 2 ** 20

time: 64.6 us -> 62.9 us (0.974)
  Pallas kernels: 62.7 us -> 61.1 us
    pallas_call x1, Pallas kernels: 62.7 us -> 61.1 us  [per_device(): pl.pallas_call(functools.partial(kernel, Z, C), out_shape=jax.ShapeDtypeS...]
where the time goes in v3:
time: 62.9 us; the launch traced here: 62.7 us
  Pallas kernels  61.1 us (97%)
  local copies, waits for them, and re-layouts  1.64 us (3%)
    pallas_call x1, Pallas kernels, per_device(): pl.pallas_call(functools.partial(kernel, Z, C), out_shape=jax.ShapeDtypeS...  61.1 us
    unnamed x1, local copies, waits for them, and re-layouts  1.64 us

profile of v3, /device:TPU:0, one launch (start us, length us, event | category | flops | bytes accessed | tf_op | source)
XLA Modules:
  0.0 62.7 jit_solution(5734352576758148629)
XLA Ops:
  0.0 61.1 %shard_map.73 = bf16[16,7168]{1,0:T(8,128)(2,1)} custom-call(s32[8]{0:T(128)} %place_ref.1, s32[4,16]{1,0:T(4,128)} %bitcast.2, bf16[4,16]{1,0:T(4,128)(2,1)} %bitcast.3, bf16[16,7168]{1,0:T(8,128)(2,1)} %tokens_ref.1, bf16[7168,512]{1,0:T(8,128)(2,1)} %wg_hbm.1, bf16[7168,512]{1,0:T(8,128)(2,1)} %wu_hbm.1, bf16[512,7168]{1,0:T(8,128)(2,1)} %wd_hbm.1), custom_call_target="tpu_custom_call" | custom-call | flops 5637144576 | bytes 22020096 | tf_op jit(solution)/shard_map/pallas_call | solution.py:243
  61.1 1.6 %copy.9 = bf16[16,7168]{1,0:T(8,128)(2,1)} copy(bf16[16,7168]{1,0:T(8,128)(2,1)} %shard_map.73) | data formatting | bytes 458752

commit v4 on v3

--- a/solution.py
+++ b/solution.py
@@ -190,10 +190,17 @@
         if step < C:
             c = step
             load_down[c].wait()
-            part = scale * jnp.dot(hid[...], wd[:, cols(c)], preferred_element_type=F32)
-            core_out[:, cols(c)] = part[half:].astype(BF16)
-            sc[c].start()
-            own[:, cols(c)] = part[:half]
+            if c == 0:
+                part = jnp.dot(hid[half:, :], wd[:, cols(c)], preferred_element_type=F32)
+                core_out[:, cols(c)] = (scale[half:] * part).astype(BF16)
+                sc[c].start()
+                part = jnp.dot(hid[0:half, :], wd[:, cols(c)], preferred_element_type=F32)
+                own[:, cols(c)] = scale[:half] * part
+            else:
+                part = scale * jnp.dot(hid[...], wd[:, cols(c)], preferred_element_type=F32)
+                core_out[:, cols(c)] = part[half:].astype(BF16)
+                sc[c].start()
+                own[:, cols(c)] = part[:half]
         if 0 <= step - 1 < C:
             c = step - 1
             sc[c].wait_recv()

time: 62.9 us -> 62.7 us (level)
  no operation moved by 1% of the time
where the time goes in v4:
time: 62.7 us; the launch traced here: 62.5 us
  Pallas kernels  60.9 us (97%)
  local copies, waits for them, and re-layouts  1.64 us (3%)
    pallas_call x1, Pallas kernels, per_device(): pl.pallas_call(functools.partial(kernel, Z, C), out_shape=jax.ShapeDtypeS...  60.9 us
    unnamed x1, local copies, waits for them, and re-layouts  1.64 us

profile of v4, /device:TPU:0, one launch (start us, length us, event | category | flops | bytes accessed | tf_op | source)
XLA Modules:
  0.0 62.5 jit_solution(3565048739997341578)
XLA Ops:
  0.0 60.9 %shard_map.73 = bf16[16,7168]{1,0:T(8,128)(2,1)} custom-call(s32[8]{0:T(128)} %place_ref.1, s32[4,16]{1,0:T(4,128)} %bitcast.2, bf16[4,16]{1,0:T(4,128)(2,1)} %bitcast.3, bf16[16,7168]{1,0:T(8,128)(2,1)} %tokens_ref.1, bf16[7168,512]{1,0:T(8,128)(2,1)} %wg_hbm.1, bf16[7168,512]{1,0:T(8,128)(2,1)} %wu_hbm.1, bf16[512,7168]{1,0:T(8,128)(2,1)} %wd_hbm.1), custom_call_target="tpu_custom_call" | custom-call | flops 5637144576 | bytes 22020096 | tf_op jit(solution)/shard_map/pallas_call | solution.py:250
  60.9 1.6 %copy.9 = bf16[16,7168]{1,0:T(8,128)(2,1)} copy(bf16[16,7168]{1,0:T(8,128)(2,1)} %shard_map.73) | data formatting | bytes 458752
